TPU v7x, 512 devices: a whole 4x4x16 slice. The times are simulated.
512 devices in a mesh: resp: 16 (over x, y_lo, core), ctx: 32 (over z, y_hi).
Axes of the slice: x: 4, y: 4 (y_hi: 2, y_lo: 2; y = y_hi * 2 + y_lo), z: 16, core: 2. Of those that a mesh axis runs over, the one named last changes fastest.
Arguments:
- queries: bfloat16 [16, 8192, 4096], P('resp', 'ctx'), may hold values from -6 to 6
- resp_kv: bfloat16 [16, 8192, 2, 512], P('resp', 'ctx'), may hold values from -6 to 6
- prompt_kv: bfloat16 [32, 128, 2, 512], P('ctx', 'resp'), may hold values from -6 to 6
- lengths: int32 [16], P('resp'), may hold values from 2048 to 8192, as said below
- block_slot: int32 [32], replicated, may hold values from 0 to 31, each once
Outputs:
- attended: bfloat16 [16, 8192, 4096], P('resp', 'ctx')
- log_total: float32 [16, 32, 8192], P('resp', None, 'ctx')
Inputs may be any that keep to these rules, and one draw needn't show every extreme that they name: `lengths`: every response has at least 2048 live positions, and some response is live over all 8192.
All inputs are finite; a program needn't handle non-finite values.
Results may differ from a plain program's by a relative error of at most 0.007.
Values may be sent and summed in bfloat16 or wider, within the bound.
A program may use at most 64 MiB of HBM per device.

v0:
```python
import math

import jax
import jax.numpy as jnp
from jax import lax
from jax.sharding import PartitionSpec as P

QUERY_HEADS = 32
KEY_VALUE_HEADS = 4
HEAD_SIZE = 128


NEGATIVE_FILL = -1e30


def shifted(block, axis, distance):
    devices = range(lax.axis_size(axis))
    route = [((i - distance) % len(devices), i) for i in devices]
    return lax.ppermute(block, axis, route)


def absorb(carried, query_tile_block, key_value_block, key_ok):
    run_max, run_total, run_sum = carried
    key_column_count = key_value_block.shape[0]
    key_matrix = key_value_block[:, 0].reshape(key_column_count, KEY_VALUE_HEADS, HEAD_SIZE)
    value_matrix = key_value_block[:, 1].reshape(key_column_count, KEY_VALUE_HEADS, HEAD_SIZE)
    scores = jnp.einsum(
        "qhgd,khd->hgqk", query_tile_block, key_matrix, preferred_element_type=jnp.float32
    )
    scores = scores * (1.0 / math.sqrt(HEAD_SIZE))
    scores = jnp.where(key_ok[None, None], scores, NEGATIVE_FILL)
    new_max = jnp.maximum(run_max, jnp.max(scores, axis=-1))
    rescale = jnp.exp(run_max - new_max)
    weights = jnp.exp(scores - new_max[..., None])
    run_total = run_total * rescale + jnp.sum(weights, axis=-1)
    added = jnp.einsum(
        "hgqk,khd->hgqd",
        weights.astype(jnp.bfloat16),
        value_matrix,
        preferred_element_type=jnp.float32,
    )
    run_sum = run_sum * rescale[..., None] + added
    return (new_max, run_total, run_sum)


def body(queries, resp_kv, prompt_kv, lengths, block_slot):
    loop_size = lax.axis_size("ctx")
    position_ctx = lax.axis_index("ctx")
    count_of_rows = queries.shape[1]
    query_group_size = QUERY_HEADS // KEY_VALUE_HEADS
    query_tile_block = queries[0].reshape(
        count_of_rows, KEY_VALUE_HEADS, query_group_size, HEAD_SIZE
    )
    local_kv = resp_kv[0]
    first_prev = shifted(local_kv, "ctx", 1)
    second_prev = shifted(first_prev, "ctx", 1)
    live_length = lengths[0]
    offsets = jnp.arange(count_of_rows, dtype=jnp.int32)
    query_pos = block_slot[position_ctx] * count_of_rows + offsets

    def response_mask(source):
        key_pos = block_slot[source] * count_of_rows + offsets
        return (key_pos[None, :] <= query_pos[:, None]) & (key_pos[None, :] < live_length)

    carried = (
        jnp.full((KEY_VALUE_HEADS, query_group_size, count_of_rows), NEGATIVE_FILL, jnp.float32),
        jnp.zeros((KEY_VALUE_HEADS, query_group_size, count_of_rows), jnp.float32),
        jnp.zeros((KEY_VALUE_HEADS, query_group_size, count_of_rows, HEAD_SIZE), jnp.float32),
    )
    piece = lax.all_gather(prompt_kv[0], "resp", axis=0, tiled=True)
    visible = jnp.ones((count_of_rows, piece.shape[0]), dtype=bool)
    carried = absorb(carried, query_tile_block, piece, visible)
    carried = absorb(carried, query_tile_block, local_kv, response_mask(position_ctx))
    carried = absorb(
        carried, query_tile_block, first_prev, response_mask((position_ctx - 1) % loop_size)
    )
    carried = absorb(
        carried, query_tile_block, second_prev, response_mask((position_ctx - 2) % loop_size)
    )
    run_max, run_total, run_sum = carried
    is_live = query_pos < live_length
    attended = run_sum / run_total[..., None]
    attended = jnp.transpose(attended, (2, 0, 1, 3)).reshape(count_of_rows, QUERY_HEADS * HEAD_SIZE)
    attended = jnp.where(is_live[:, None], attended, 0.0).astype(jnp.bfloat16)
    log_total = (run_max + jnp.log(run_total)).reshape(QUERY_HEADS, count_of_rows)
    log_total = jnp.where(is_live[None, :], log_total, 0.0)
    return (attended[None], log_total[None])


def solution(mesh):
    return jax.shard_map(
        body,
        mesh=mesh,
        in_specs=(
            P("resp", "ctx", None),
            P("resp", "ctx", None, None),
            P("ctx", "resp", None, None),
            P("resp"),
            P(),
        ),
        out_specs=(P("resp", "ctx", None), P("resp", None, "ctx")),
        check_vma=False,
    )
```

profile of v0, /device:TPU:1, one launch (start us, length us, event | category | flops | bytes accessed | tf_op | source)
XLA Modules:
  0.0 94.2 jit_solution(6451615173308403907)
XLA Ops:
  0.6 1.4 %copy.40 = bf16[1,256,2,512]{1,3,2,0:T(8,128)(2,1)S(1)} copy(bf16[1,256,2,512]{3,2,1,0:T(2,128)(2,1)} %param.6) | data formatting | bytes 1048576 | tf_op args[1]
  2.1 5.7 %collective-permute-start = (bf16[256,2,512]{0,2,1:T(8,128)(2,1)S(1)}, bf16[256,2,512]{0,2,1:T(8,128)(2,1)}, u32[]{:S(2)}, u32[]{:S(2)}) collective-permute-start(bf16[256,2,512]{0,2,1:T(8,128)(2,1)S(1)} %bitcast.254), channel_id=1, source_target_pairs={{31,0},{0,1},{1,2},{2,3},{3,4},{4,5},{5,6},{6,7},{7,8},{8,9},{9,10... | collective-permute-start | bytes 1572872 | tf_op jit(solution)/shard_map/ppermute | solution.py:19
  7.8 0.7 fusion.78
  9.2 1.4 %fusion.81 = (s32[1]{0:T(128)}, s32[1]{0:T(128)}, s32[1]{0:T(128)}) fusion(s32[32]{0:T(128)} %param.9, s32[]{:T(128)S(6)} %select_n.58, s32[]{:T(128)S(6)} %select_n.55, s32[]{:T(128)S(6)} %select_n.61), kind=kLoop, calls=%fused_computation.115 | loop fusion | bytes 36 | tf_op jit(solution)/shard_map/dynamic_slice | solution.py:62
  13.1 22.1 %all-gather = bf16[1,128,2,512]{3,2,0,1:T(2,128)(2,1)S(1)} all-gather(bf16[1,8,2,512]{3,2,0,1:T(2,128)(2,1)} %bitcast.265), channel_id=2, replica_groups=mesh['resp'=16,'ctx'=32] {'resp'}, dimensions={1}, use_global_device_ids=true | all-gather | bytes 278528 | tf_op jit(solution)/shard_map/all_gather | solution.py:70
  36.0 1.5 %bitcast_reduce_fusion = (f32[4,8,256]{2,1,0:T(8,128)S(1)}, f32[4,128,256,8]{2,1,3,0:T(8,128)S(1)}) fusion(bf16[128,4,128,1]{0,2,3,1:T(8,128)(2,1)S(1)} %bitcast.263, bf16[256,4,8,128]{3,2,1,0:T(8,128)(2,1)S(1)} %bitcast.248), kind=kOutput, calls=%fused_computation.27 | convolution fusion | flops 270524416 | bytes 6455296 | tf_op jit(solution)/shard_map/qhgd,khd->hgqk/dot_general | solution.py:27
  37.8 2.3 %fusion.6 = (f32[4,8,256]{2,1,0:T(8,128)S(1)}, f32[4,256,256,8]{2,1,3,0:T(8,128)S(1)}) fusion(pred[256,256]{0,1:T(8,128)(4,1)S(1)} %get-tuple-element.19, bf16[256,4,128,1]{0,2,3,1:T(8,128)(2,1)S(1)} %bitcast.259, bf16[256,4,8,128]{3,2,1,0:T(8,128)(2,1)S(1)} %bitcast.249), kind=kOutput, calls=%fused_computation.12 | convolution fusion | flops 543154176 | bytes 10846208 | tf_op jit(solution)/shard_map/qhgd,khd->hgqk/dot_general | solution.py:27
  40.1 11.0 %collective-permute-start.1 = (bf16[256,2,512]{0,2,1:T(8,128)(2,1)}, bf16[256,2,512]{0,2,1:T(8,128)(2,1)S(1)}, u32[]{:S(2)}, u32[]{:S(2)}) collective-permute-start(bf16[256,2,512]{0,2,1:T(8,128)(2,1)} %collective-permute-done), channel_id=1, source_target_pairs={{31,0},{0,1},{1,2},{2,3},{3,4},{4,5},{5,6},{6,7},{7,8},{8,9},{9,10... | collective-permute-start | bytes 1572872 | tf_op jit(solution)/shard_map/ppermute | solution.py:19
  51.2 1.1 %fusion.79 = (bf16[256,1,512]{0,2,1:T(8,128)(2,1)S(1)}, bf16[256,1,512]{0,2,1:T(8,128)(2,1)S(1)}) fusion(bf16[256,2,512]{0,2,1:T(8,128)(2,1)} %collective-permute-done), kind=kLoop, calls=%fused_computation.113 | loop fusion | bytes 1048576 | tf_op jit(solution)/shard_map/slice | solution.py:25
  52.2 2.3 %fusion.7 = (f32[4,8,256]{2,1,0:T(8,128)S(1)}, f32[4,256,256,8]{2,1,3,0:T(8,128)S(1)}) fusion(pred[256,256]{0,1:T(8,128)(4,1)S(1)} %get-tuple-element.20, bf16[256,4,128,1]{0,2,3,1:T(8,128)(2,1)S(1)} %bitcast.261, bf16[256,4,8,128]{3,2,1,0:T(8,128)(2,1)S(1)} %bitcast.250), kind=kOutput, calls=%fused_computation.13 | convolution fusion | flops 543154176 | bytes 10846208 | tf_op jit(solution)/shard_map/qhgd,khd->hgqk/dot_general | solution.py:27
  54.6 9.8 %collective-permute-done.1 = bf16[256,2,512]{0,2,1:T(8,128)(2,1)S(1)} collective-permute-done((bf16[256,2,512]{0,2,1:T(8,128)(2,1)}, bf16[256,2,512]{0,2,1:T(8,128)(2,1)S(1)}, u32[]{:S(2)}, u32[]{:S(2)}) %collective-permute-start.1) | collective-permute-done | bytes 524320 | tf_op jit(solution)/shard_map/ppermute | solution.py:19
  64.3 0.7 fusion.77
  65.1 2.3 %fusion.8 = (f32[4,8,256]{2,1,0:T(8,128)S(1)}, f32[4,256,256,8]{2,1,3,0:T(8,128)S(1)}) fusion(pred[256,256]{0,1:T(8,128)(4,1)S(1)} %get-tuple-element.21, bf16[256,4,128,1]{0,2,3,1:T(8,128)(2,1)S(1)} %bitcast.260, bf16[256,4,8,128]{3,2,1,0:T(8,128)(2,1)S(1)} %bitcast.251), kind=kOutput, calls=%fused_computation.14 | convolution fusion | flops 543154176 | bytes 10846208 | tf_op jit(solution)/shard_map/qhgd,khd->hgqk/dot_general | solution.py:27
  67.5 1.9 %fusion.4 = f32[4,8,256]{2,1,0:T(8,128)S(1)} fusion(f32[4,256,256,8]{2,1,3,0:T(8,128)S(1)} %get-tuple-element.26, f32[4,8,256]{2,1,0:T(8,128)S(1)} %get-tuple-element.5, pred[256,256]{0,1:T(8,128)(4,1)S(1)} %get-tuple-element.21), kind=kLoop, calls=%fused_computation.10 | loop fusion | flops 8380416 | bytes 8519680 | tf_op jit(solution)/shard_map/reduce_sum | solution.py:35
  69.3 1.9 %fusion.2 = f32[4,8,256]{2,1,0:T(8,128)S(1)} fusion(f32[4,256,256,8]{2,1,3,0:T(8,128)S(1)} %get-tuple-element.28, f32[4,8,256]{2,1,0:T(8,128)S(1)} %get-tuple-element.6, pred[256,256]{0,1:T(8,128)(4,1)S(1)} %get-tuple-element.20), kind=kLoop, calls=%fused_computation.8 | loop fusion | flops 8380416 | bytes 8519680 | tf_op jit(solution)/shard_map/reduce_sum | solution.py:35
  71.2 2.5 %fusion = f32[4,8,256]{2,1,0:T(8,128)} fusion(f32[4,256,256,8]{2,1,3,0:T(8,128)S(1)} %get-tuple-element.30, f32[4,8,256]{2,1,0:T(8,128)S(1)} %get-tuple-element.7, pred[256,256]{0,1:T(8,128)(4,1)S(1)} %get-tuple-element.19), kind=kLoop, calls=%fused_computation.6 | loop fusion | flops 8380416 | bytes 8519680 | tf_op jit(solution)/shard_map/reduce_sum | solution.py:35
  73.7 0.8 fusion.32
  75.9 4.4 %fusion.11 = f32[4,8,256,128]{2,3,1,0:T(8,128)} fusion(bf16[256,4,128,1]{0,2,3,1:T(8,128)(2,1)S(1)} %bitcast.257, f32[4,256,256,8]{2,1,3,0:T(8,128)S(1)} %get-tuple-element.28, f32[4,8,256]{2,1,0:T(8,128)S(1)} %get-tuple-element.6, pred[256,256]{0,1:T(8,128)(4,1)S(1)} %get-tuple-element.20), kind=kOutput, calls=%fused_computation.16 | convolution fusion | flops 545259520 | bytes 12943360 | tf_op jit(solution)/shard_map/hgqk,khd->hgqd/dot_general | solution.py:36
  80.2 2.3 %fusion.13 = f32[4,8,256,128]{2,3,1,0:T(8,128)S(1)} fusion(bf16[256,4,128,1]{0,2,3,1:T(8,128)(2,1)S(1)} %bitcast.256, f32[4,256,256,8]{2,1,3,0:T(8,128)S(1)} %get-tuple-element.30, f32[4,8,256]{2,1,0:T(8,128)S(1)} %get-tuple-element.7, pred[256,256]{0,1:T(8,128)(4,1)S(1)} %get-tuple-element.19), kind=kOutput, calls=%fused_computation.17 | convolution fusion | flops 545259520 | bytes 12943360 | tf_op jit(solution)/shard_map/hgqk,khd->hgqd/dot_general | solution.py:36
  82.6 0.9 fusion.34
  83.4 1.2 %copy-done = f32[4,8,256,128]{2,3,1,0:T(8,128)S(1)} copy-done((f32[4,8,256,128]{2,3,1,0:T(8,128)S(1)}, f32[4,8,256,128]{2,3,1,0:T(8,128)}, u32[]{:S(2)}) %copy-start) | copy-done | bytes 4194328
  84.7 4.6 %fusion.15 = bf16[256,4,8,128]{0,3,2,1:T(8,128)(2,1)} fusion(f32[4,8,256,128]{2,3,1,0:T(8,128)S(1)} %copy-done, f32[4,8,256,128]{2,3,1,0:T(8,128)S(1)} %fusion.13, f32[4,8,256,128]{2,3,1,0:T(8,128)S(1)} %fusion.34, f32[256,4,8]{0,2,1:T(8,128)S(1)} %copy-done.7, f32[256,4,8]{0,2,1:T(8,128)S(1)} %copy-done.9, f32[256,4,8]{0,2,1:T(8,128)S(1)} %copy-done.8, ...), kind=kOutput, calls=%fused_computation.19 | convolution fusion | flops 554696704 | bytes 23592960 | tf_op jit(solution)/shard_map/hgqk,khd->hgqd/dot_general | solution.py:36
  89.4 2.9 %copy.50 = bf16[1,256,4096]{2,1,0:T(8,128)(2,1)S(1)} copy(bf16[1,256,4096]{1,2,0:T(8,128)(2,1)} %bitcast.253) | data formatting | bytes 4194304 | tf_op jit(solution)/shard_map/reshape | solution.py:83
  92.3 1.9 %select_convert_fusion = bf16[1,256,4096]{2,1,0:T(8,128)(2,1)} fusion(bf16[1,256,4096]{2,1,0:T(8,128)(2,1)S(1)} %copy.50, pred[256]{0:T(512)(128)(4,1)S(1)} %broadcast_compare_fusion.2), kind=kLoop, calls=%fused_computation.29 | loop fusion | flops 1048576 | bytes 4194560 | tf_op jit(solution)/shard_map/convert_element_type | solution.py:84
  (39 shorter events, 3.0 us)
Async XLA Ops:
  0.6 34.8 %copy-start.1 = (bf16[1,256,4096]{2,1,0:T(8,128)(2,1)S(1)}, bf16[1,256,4096]{2,1,0:T(8,128)(2,1)}, u32[]{:S(2)}) copy-start(bf16[1,256,4096]{2,1,0:T(8,128)(2,1)} %param.5) | copy-start | bytes 6291460
  2.1 38.0 %collective-permute-start = (bf16[256,2,512]{0,2,1:T(8,128)(2,1)S(1)}, bf16[256,2,512]{0,2,1:T(8,128)(2,1)}, u32[]{:S(2)}, u32[]{:S(2)}) collective-permute-start(bf16[256,2,512]{0,2,1:T(8,128)(2,1)S(1)} %bitcast.254), channel_id=1, source_target_pairs={{31,0},{0,1},{1,2},{2,3},{3,4},{4,5},{5,6},{6,7},{7,8},{8,9},{9,10... | collective-permute-start | bytes 1572872 | tf_op jit(solution)/shard_map/ppermute | solution.py:19
  36.0 1.5 %copy-start.12 = (pred[256]{0:T(512)(128)(4,1)S(1)}, pred[256]{0:T(512)(128)(4,1)}, u32[]{:S(2)}) copy-start(pred[256]{0:T(512)(128)(4,1)} %get-tuple-element.33) | copy-start | bytes 772
  36.0 1.5 %copy-start.13 = (pred[256]{0:T(512)(128)(4,1)S(1)}, pred[256]{0:T(512)(128)(4,1)}, u32[]{:S(2)}) copy-start(pred[256]{0:T(512)(128)(4,1)} %get-tuple-element.34) | copy-start | bytes 772
  36.0 1.8 %copy-start.2 = (bf16[256,1,512]{0,2,1:T(8,128)(2,1)S(1)}, bf16[256,1,512]{0,2,1:T(8,128)(2,1)}, u32[]{:S(2)}) copy-start(bf16[256,1,512]{0,2,1:T(8,128)(2,1)} %get-tuple-element.11) | copy-start | bytes 786436
  40.1 24.2 %collective-permute-start.1 = (bf16[256,2,512]{0,2,1:T(8,128)(2,1)}, bf16[256,2,512]{0,2,1:T(8,128)(2,1)S(1)}, u32[]{:S(2)}, u32[]{:S(2)}) collective-permute-start(bf16[256,2,512]{0,2,1:T(8,128)(2,1)} %collective-permute-done), channel_id=1, source_target_pairs={{31,0},{0,1},{1,2},{2,3},{3,4},{4,5},{5,6},{6,7},{7,8},{8,9},{9,10... | collective-permute-start | bytes 1572872 | tf_op jit(solution)/shard_map/ppermute | solution.py:19
  67.4 1.9 %copy-start.5 = (f32[4,8,256]{2,1,0:T(8,128)}, f32[4,8,256]{2,1,0:T(8,128)S(1)}, u32[]{:S(2)}) copy-start(f32[4,8,256]{2,1,0:T(8,128)S(1)} %get-tuple-element.5) | copy-start | bytes 98308
  73.7 0.8 copy-start.3
  82.5 2.2 %copy-start = (f32[4,8,256,128]{2,3,1,0:T(8,128)S(1)}, f32[4,8,256,128]{2,3,1,0:T(8,128)}, u32[]{:S(2)}) copy-start(f32[4,8,256,128]{2,3,1,0:T(8,128)} %fusion.11) | copy-start | bytes 12582916
  82.5 2.2 %copy-start.4 = (bf16[256,1,512]{0,2,1:T(8,128)(2,1)S(1)}, bf16[256,1,512]{0,2,1:T(8,128)(2,1)}, u32[]{:S(2)}) copy-start(bf16[256,1,512]{0,2,1:T(8,128)(2,1)} %get-tuple-element.8) | copy-start | bytes 786436
  82.5 2.2 %copy-start.6 = (f32[4,8,256]{2,1,0:T(8,128)S(1)}, f32[4,8,256]{2,1,0:T(8,128)}, u32[]{:S(2)}) copy-start(f32[4,8,256]{2,1,0:T(8,128)} %copy-done.5) | copy-start | bytes 98308
  82.5 2.2 %copy-start.7 = (f32[256,4,8]{0,2,1:T(8,128)S(1)}, f32[256,4,8]{0,2,1:T(8,128)}, u32[]{:S(2)}) copy-start(f32[256,4,8]{0,2,1:T(8,128)} %get-tuple-element.2) | copy-start | bytes 98308
  82.5 2.2 %copy-start.8 = (f32[256,4,8]{0,2,1:T(8,128)S(1)}, f32[256,4,8]{0,2,1:T(8,128)}, u32[]{:S(2)}) copy-start(f32[256,4,8]{0,2,1:T(8,128)} %get-tuple-element.3) | copy-start | bytes 98308
  82.6 2.2 %copy-start.9 = (f32[256,4,8]{0,2,1:T(8,128)S(1)}, f32[256,4,8]{0,2,1:T(8,128)}, u32[]{:S(2)}) copy-start(f32[256,4,8]{0,2,1:T(8,128)} %get-tuple-element.4) | copy-start | bytes 98308
  82.6 2.2 %copy-start.10 = (f32[256,4,8]{0,2,1:T(8,128)S(1)}, f32[256,4,8]{0,2,1:T(8,128)}, u32[]{:S(2)}) copy-start(f32[256,4,8]{0,2,1:T(8,128)} %get-tuple-element.16) | copy-start | bytes 98308
  82.6 2.2 %copy-start.11 = (f32[256,4,8]{0,2,1:T(8,128)S(1)}, f32[256,4,8]{0,2,1:T(8,128)}, u32[]{:S(2)}) copy-start(f32[256,4,8]{0,2,1:T(8,128)} %get-tuple-element.17) | copy-start | bytes 98308
where the time goes:
time: 94.5 us; the launch traced here: 94.2 us
  blocking collectives  22.1 us (23%)
  matrix products  20.6 us (22%)
  starting transfers between devices  16.7 us (18%)
  other arithmetic  11.1 us (12%)
  local copies, waits for them, and re-layouts  10.3 us (11%)
  waiting for transfers between devices  9.77 us (10%)
  between operations  3.58 us (4%)
    all_gather x1, blocking collectives, body(): piece = lax.all_gather(prompt_kv[0], 'resp', axis=0, tiled=True)  22.1 us
    ppermute x2, starting transfers between devices, shifted(): return lax.ppermute(block, axis, route)  16.7 us
    dot_general x4, matrix products, absorb(): jnp.einsum('hgqk,khd->hgqd', weights.astype(jnp.bfloat16), value_matrix,...  12.1 us
    ppermute x2, waiting for transfers between devices, shifted(): return lax.ppermute(block, axis, route)  9.77 us
    dot_general x4, matrix products, absorb(): jnp.einsum('qhgd,khd->hgqk', query_tile_block, key_matrix, preferred_elem...  8.47 us
    reduce_sum x4, other arithmetic, absorb(): run_total = run_total * rescale + jnp.sum(weights, axis=-1)  7.02 us
    unnamed x30, local copies, waits for them, and re-layouts  3.24 us
    reshape x1, local copies, waits for them, and re-layouts, body(): jnp.transpose(attended, (2, 0, 1, 3))  2.91 us
  transfers between devices with their start and end apart: 2, of which 1 were waited for; matrix products, arithmetic and copies ran while one was open for 12% of the time, Pallas kernels for 0%

commit v1 on v0

v1 whole, which is shorter than its diff:
```python
import math

import jax
import jax.numpy as jnp
from jax import lax
from jax.experimental import pallas as pl
from jax.experimental.pallas import tpu as pltpu
from jax.sharding import PartitionSpec as P

QUERY_HEADS = 32
KEY_VALUE_HEADS = 4
GROUP = QUERY_HEADS // KEY_VALUE_HEADS
HEAD_SIZE = 128
ROWS = 256
PROMPT = 128
NEAR = ROWS + PROMPT
N_CTX = 32
N_RESP = 16
NEGATIVE_FILL = -1e30
LOG2_SCALE = math.log2(math.e) / math.sqrt(HEAD_SIZE)
LN2 = math.log(2.0)
F32 = jnp.float32
BF16 = jnp.bfloat16
NT = (((1,), (1,)), ((), ()))
MESH = pl.DeviceIdType.MESH


def at(resp, ctx):
    return {"resp": resp, "ctx": ctx}


def remote(src, dst, send_sem, recv_sem, target):
    return pltpu.make_async_remote_copy(
        src_ref=src,
        dst_ref=dst,
        send_sem=send_sem,
        recv_sem=recv_sem,
        device_id=target,
        device_id_type=MESH,
    )


def head_columns(head):
    return pl.ds(pl.multiple_of(head * HEAD_SIZE, HEAD_SIZE), HEAD_SIZE)


def kernel(
    q_hbm, kv_hbm, prompt_hbm, length_ref, slot_ref,
    out_ref, log_ref,
    q, kv_raw, prompt_raw, near_k, near_v, z_k, z_v, y_k, y_v,
    near_bias, near_top, near_sum, top_all, total_all,
    near_s, near_p, far_s, far_p,
    q_sem, kv_sem, own_sem, z_send, z_recv, y_send, y_recv,
    first_send, first_recv, second_send, second_recv, third_send, third_recv,
):
    r = lax.axis_index("resp")
    c = lax.axis_index("ctx")
    core = lax.rem(r, 2)
    pair = r // 2
    odd = lax.rem(c, 2)
    next_z = at(r, lax.rem(c + 2, N_CTX))
    prev_z = at(r, lax.rem(c + N_CTX - 2, N_CTX))
    across = at(r, c + 1 - 2 * odd)
    sibling = at(r + 1 - 2 * core, c)
    y_side = at(r + 2 - 4 * lax.rem(pair, 2), c)
    x_peers = [at(lax.rem(r + 4 * k, N_RESP), c) for k in (1, 2, 3)]

    barrier = pltpu.get_barrier_semaphore()
    for device in (prev_z, across, sibling, y_side, *x_peers):
        pl.semaphore_signal(barrier, inc=1, device_id=device, device_id_type=MESH)

    kv_copies = [
        pltpu.make_async_copy(
            kv_hbm.at[:, :, pl.ds(g * HEAD_SIZE, HEAD_SIZE)], kv_raw.at[g], kv_sem.at[g]
        )
        for g in range(KEY_VALUE_HEADS)
    ]
    for copy in kv_copies:
        copy.start()
    own_place = pl.ds((core * 8 + pair) * 8, 8)
    own_copy = pltpu.make_async_copy(prompt_hbm, prompt_raw.at[own_place], own_sem)
    own_copy.start()
    q_copy = pltpu.make_async_copy(q_hbm, q, q_sem)
    q_copy.start()

    def z_copies(g):
        return (
            remote(near_k.at[g, pl.ds(0, ROWS)], z_k.at[g], z_send.at[2 * g], z_recv.at[2 * g], next_z),
            remote(near_v.at[g, pl.ds(0, ROWS)], z_v.at[g], z_send.at[2 * g + 1], z_recv.at[2 * g + 1], next_z),
        )

    def y_copies(g, k_from, v_from):
        return (
            remote(k_from, y_k.at[g], y_send.at[2 * g], y_recv.at[2 * g], across),
            remote(v_from, y_v.at[g], y_send.at[2 * g + 1], y_recv.at[2 * g + 1], across),
        )

    def own_y_copies(g):
        return y_copies(g, near_k.at[g, pl.ds(0, ROWS)], near_v.at[g, pl.ds(0, ROWS)])

    for g in range(KEY_VALUE_HEADS):
        kv_copies[g].wait()
        both = kv_raw[g].astype(F32)
        near_k[g, 0:ROWS] = both[:, 0].astype(BF16)
        near_v[g, 0:ROWS] = both[:, 1].astype(BF16)
        if g == 0:
            pl.semaphore_wait(barrier, 7)
        for copy in z_copies(g):
            copy.start()

        @pl.when(odd == 0)
        def _():
            for copy in own_y_copies(g):
                copy.start()

    own_copy.wait()
    side_pair = pair + 1 - 2 * lax.rem(pair, 2)
    side_place = pl.ds((core * 8 + side_pair) * 8, 8)
    own_rows = prompt_raw.at[own_place]
    side_rows = prompt_raw.at[side_place]
    first = [
        remote(own_rows, own_rows, first_send.at[k], first_recv.at[k], target)
        for k, target in enumerate((y_side, *x_peers))
    ]
    second = [
        remote(side_rows, side_rows, second_send.at[k], second_recv.at[k], target)
        for k, target in enumerate(x_peers)
    ]
    half = prompt_raw.at[pl.ds(core * 64, 64)]
    third = remote(half, half, third_send, third_recv, sibling)
    for copy in first:
        copy.start()

    slot = slot_ref[c]
    live_length = length_ref[0]
    row = lax.broadcasted_iota(jnp.int32, (ROWS, ROWS), 0)
    column = lax.broadcasted_iota(jnp.int32, (ROWS, ROWS), 1)
    near_ok = (column <= row) & (slot * ROWS + column < live_length)
    near_bias[...] = jnp.where(near_ok, 0.0, NEGATIVE_FILL)

    first[0].wait_recv()
    for copy in second:
        copy.start()
    for copy in (*first[1:], *second):
        copy.wait_recv()
    third.start()
    for copy in (*first, *second):
        copy.wait_send()
    third.wait()
    rows = prompt_raw[...].astype(F32)
    for g in range(KEY_VALUE_HEADS):
        lanes = slice(g * HEAD_SIZE, (g + 1) * HEAD_SIZE)
        near_k[g, ROWS:NEAR] = rows[:, 0, lanes].astype(BF16)
        near_v[g, ROWS:NEAR] = rows[:, 1, lanes].astype(BF16)
    q_copy.wait()

    lane = lax.broadcasted_iota(jnp.int32, (ROWS, HEAD_SIZE), 1)
    ones = jnp.ones((ROWS, HEAD_SIZE), BF16)
    top_all[...] = jnp.zeros_like(top_all)
    total_all[...] = jnp.ones_like(total_all)

    def pipelined(scores, soften, weigh):
        for step in range(GROUP + 2):
            if step < GROUP:
                scores(step)
            if 1 <= step <= GROUP:
                soften(step - 1)
            if step >= 2:
                weigh(step - 2)

    @pl.loop(0, KEY_VALUE_HEADS)
    def _(g):
        def scores(i):
            near_s[i % 2] = lax.dot_general(
                q[:, head_columns(g * GROUP + i)], near_k[g], NT, preferred_element_type=F32
            )

        def soften(i):
            s = near_s[i % 2] * LOG2_SCALE
            s = jnp.concatenate([s[:, :ROWS] + near_bias[...], s[:, ROWS:]], axis=1)
            top = jnp.max(s, axis=1, keepdims=True)
            near_p[i % 2] = jnp.exp2(s - top).astype(BF16)
            near_top[g * GROUP + i] = jnp.broadcast_to(top, (ROWS, HEAD_SIZE))

        def weigh(i):
            v = jnp.concatenate(
                [near_v[g], jnp.ones((NEAR, HEAD_SIZE), BF16)], axis=1
            )
            near_sum[g * GROUP + i] = jnp.dot(near_p[i % 2], v, preferred_element_type=F32)

        pipelined(scores, soften, weigh)

    key = lax.broadcasted_iota(jnp.int32, (1, ROWS), 1)

    def far_bias(back):
        source_slot = slot_ref[lax.rem(c + N_CTX - back, N_CTX)]
        ok = (source_slot * ROWS + key < live_length) & (source_slot < slot)
        return jnp.where(ok, 0.0, NEGATIVE_FILL)

    bias = jnp.concatenate([far_bias(2), far_bias(1)], axis=1)
    query = lax.broadcasted_iota(jnp.int32, (ROWS, HEAD_SIZE), 0)
    is_live = slot * ROWS + query < live_length

    @pl.loop(0, KEY_VALUE_HEADS)
    def _(g):
        forward = y_copies(g, z_k.at[g], z_v.at[g])
        for arriving, onward in zip(z_copies(g), forward, strict=True):
            arriving.wait_recv()

            @pl.when(odd == 1)
            def _():
                onward.start()

        for arriving in forward:
            arriving.wait_recv()

        def scores(i):
            one = q[:, head_columns(g * GROUP + i)]
            far_s[i % 2, :, 0:ROWS] = lax.dot_general(one, z_k[g], NT, preferred_element_type=F32)
            far_s[i % 2, :, ROWS:] = lax.dot_general(one, y_k[g], NT, preferred_element_type=F32)

        def soften(i):
            head = g * GROUP + i
            s = far_s[i % 2] * LOG2_SCALE + bias
            before = near_top[head]
            top = jnp.maximum(before, jnp.max(s, axis=1, keepdims=True))
            far_p[i % 2] = jnp.exp2(s - jnp.concatenate([top] * 4, axis=1)).astype(BF16)
            near_top[head] = jnp.exp2(before - top)
            top_all[...] = jnp.where(lane == head, top, top_all[...])

        def weigh(i):
            head = g * GROUP + i
            v = jnp.concatenate(
                [
                    jnp.concatenate([z_v[g], ones], axis=1),
                    jnp.concatenate([y_v[g], ones], axis=1),
                ],
                axis=0,
            )
            added = jnp.dot(far_p[i % 2], v, preferred_element_type=F32)
            rescale = near_top[head]
            near = near_sum[head]
            total = near[:, HEAD_SIZE:] * rescale + added[:, HEAD_SIZE:]
            summed = near[:, :HEAD_SIZE] * rescale + added[:, :HEAD_SIZE]
            attended = jnp.where(is_live, summed * (1.0 / total), 0.0)
            out_ref[:, head_columns(head)] = attended.astype(BF16)
            total_all[...] = jnp.where(lane == head, total, total_all[...])

        pipelined(scores, soften, weigh)

    log_total = ((top_all[...] + jnp.log2(total_all[...])) * LN2).T[:QUERY_HEADS]
    place = lax.broadcasted_iota(jnp.int32, (QUERY_HEADS, ROWS), 1)
    log_ref[...] = jnp.where(slot * ROWS + place < live_length, log_total, 0.0)

    for g in range(KEY_VALUE_HEADS):
        for copy in (*z_copies(g), *own_y_copies(g)):
            copy.wait_send()


def body(queries, resp_kv, prompt_kv, lengths, block_slot):
    hbm = pl.BlockSpec(memory_space=pltpu.HBM)
    smem = pl.BlockSpec(memory_space=pltpu.SMEM)
    vmem = pl.BlockSpec(memory_space=pltpu.VMEM)
    dma = pltpu.SemaphoreType.DMA
    block = pltpu.VMEM((KEY_VALUE_HEADS, ROWS, HEAD_SIZE), BF16)
    near = pltpu.VMEM((KEY_VALUE_HEADS, NEAR, HEAD_SIZE), BF16)
    attended, log_total = pl.pallas_call(
        kernel,
        out_shape=(
            jax.ShapeDtypeStruct((ROWS, QUERY_HEADS * HEAD_SIZE), BF16),
            jax.ShapeDtypeStruct((QUERY_HEADS, ROWS), F32),
        ),
        in_specs=[hbm, hbm, hbm, smem, smem],
        out_specs=(vmem, vmem),
        scratch_shapes=[
            pltpu.VMEM((ROWS, QUERY_HEADS * HEAD_SIZE), BF16),
            pltpu.VMEM((KEY_VALUE_HEADS, ROWS, 2, HEAD_SIZE), BF16),
            pltpu.VMEM((PROMPT, 2, KEY_VALUE_HEADS * HEAD_SIZE), BF16),
            near, near, block, block, block, block,
            pltpu.VMEM((ROWS, ROWS), F32),
            pltpu.VMEM((QUERY_HEADS, ROWS, HEAD_SIZE), F32),
            pltpu.VMEM((QUERY_HEADS, ROWS, 2 * HEAD_SIZE), F32),
            pltpu.VMEM((ROWS, HEAD_SIZE), F32),
            pltpu.VMEM((ROWS, HEAD_SIZE), F32),
            pltpu.VMEM((2, ROWS, NEAR), F32),
            pltpu.VMEM((2, ROWS, NEAR), BF16),
            pltpu.VMEM((2, ROWS, 2 * ROWS), F32),
            pltpu.VMEM((2, ROWS, 2 * ROWS), BF16),
            dma, dma((4,)), dma, dma((8,)), dma((8,)), dma((8,)), dma((8,)),
            dma((4,)), dma((4,)), dma((3,)), dma((3,)), dma, dma,
        ],
        compiler_params=pltpu.CompilerParams(
            collective_id=0, has_side_effects=True, vmem_limit_bytes=63 * 1024 * 1024
        ),
    )(queries[0], resp_kv[0], prompt_kv[0], lengths, block_slot)
    return attended[None], log_total[None]


def solution(mesh):
    return jax.shard_map(
        body,
        mesh=mesh,
        in_specs=(
            P("resp", "ctx", None),
            P("resp", "ctx", None, None),
            P("ctx", "resp", None, None),
            P("resp"),
            P(),
        ),
        out_specs=(P("resp", "ctx", None), P("resp", None, "ctx")),
        check_vma=False,
    )
```

time: 94.5 us -> 44.8 us (0.47)
  the two profiles are of different devices: /device:TPU:1 before, /device:TPU:96 now
where the time goes in v1:
time: 44.8 us; the launch traced here: 44.6 us
  Pallas kernels  39.6 us (88%)
  local copies, waits for them, and re-layouts  3.75 us (8%)
  between operations  1.29 us (3%)
    pallas_call x1, Pallas kernels, body(): pl.pallas_call(kernel, out_shape=(jax.ShapeDtypeStruct((ROWS, QUERY_HEADS...  39.6 us
    unnamed x4, local copies, waits for them, and re-layouts  3.75 us

profile of v1, /device:TPU:96, one launch (start us, length us, event | category | flops | bytes accessed | tf_op | source)
XLA Modules:
  0.0 44.6 jit_solution(142808819998707724)
XLA Ops:
  1.3 39.6 %shard_map.68 = (bf16[256,4096]{1,0:T(8,128)(2,1)}, f32[32,256]{1,0:T(8,128)}) custom-call(bf16[256,4096]{1,0:T(8,128)(2,1)} %bitcast.5, bf16[256,2,512]{2,1,0:T(2,128)(2,1)} %bitcast.7, bf16[8,2,512]{2,1,0:T(2,128)(2,1)} %bitcast.9, s32[1]{0:T(128)S(6)} %copy.9.length_ref, s32[32]{0:T(128)} %slot_ref.1), custom_call_target="tpu_custom_call" | custom-call | tf_op jit(solution)/shard_map/pallas_call | solution.py:267
  40.9 0.0 copy-start
  40.9 3.1 %copy.10 = bf16[1,256,4096]{2,1,0:T(8,128)(2,1)} copy(bf16[1,256,4096]{2,1,0:T(8,128)(2,1)} %bitcast.6) | data formatting | bytes 4194304
  44.0 0.0 copy-done
  44.0 0.6 %copy.11 = f32[1,32,256]{2,1,0:T(8,128)} copy(f32[1,32,256]{2,1,0:T(8,128)S(1)} %bitcast.8) | data formatting | bytes 65536
Async XLA Ops:
  40.9 3.1 %copy-start = (f32[32,256]{1,0:T(8,128)S(1)}, f32[32,256]{1,0:T(8,128)}, u32[]{:S(2)}) copy-start(f32[32,256]{1,0:T(8,128)} %get-tuple-element.5) | copy-start | bytes 98308

commit v2 on v1

v2 whole, which is shorter than its diff:
```python
import math

import jax
import jax.numpy as jnp
from jax import lax
from jax.experimental import pallas as pl
from jax.experimental.pallas import tpu as pltpu
from jax.sharding import PartitionSpec as P

QUERY_HEADS = 32
KEY_VALUE_HEADS = 4
GROUP = QUERY_HEADS // KEY_VALUE_HEADS
HEAD_SIZE = 128
ROWS = 256
PROMPT = 128
LAST = ROWS + PROMPT
N_CTX = 32
N_RESP = 16
NEGATIVE_FILL = -1e30
LOG2_SCALE = math.log2(math.e) / math.sqrt(HEAD_SIZE)
LN2 = math.log(2.0)
F32 = jnp.float32
BF16 = jnp.bfloat16
NT = (((1,), (1,)), ((), ()))
MESH = pl.DeviceIdType.MESH


def at(resp, ctx):
    return {"resp": resp, "ctx": ctx}


def remote(src, dst, send_sem, recv_sem, target):
    return pltpu.make_async_remote_copy(
        src_ref=src,
        dst_ref=dst,
        send_sem=send_sem,
        recv_sem=recv_sem,
        device_id=target,
        device_id_type=MESH,
    )


def head_columns(head):
    return pl.ds(pl.multiple_of(head * HEAD_SIZE, HEAD_SIZE), HEAD_SIZE)


def kernel(
    q_hbm, kv_hbm, prompt_hbm, length_ref, slot_ref,
    out_ref, log_ref,
    q, kv_raw, prompt_raw, own_k, own_v, other_k, other_v,
    near_bias, top_of, sum_of, top_all, total_all, score, weight, out,
    q_sem, kv_sem, own_sem, z_send, z_recv, y_send, y_recv,
    first_send, first_recv, second_send, second_recv, third_send, third_recv, out_sem,
):
    r = lax.axis_index("resp")
    c = lax.axis_index("ctx")
    core = lax.rem(r, 2)
    pair = r // 2
    odd = lax.rem(c, 2)
    next_z = at(r, lax.rem(c + 2, N_CTX))
    prev_z = at(r, lax.rem(c + N_CTX - 2, N_CTX))
    across = at(r, c + 1 - 2 * odd)
    sibling = at(r + 1 - 2 * core, c)
    y_side = at(r + 2 - 4 * lax.rem(pair, 2), c)
    x_peers = [at(lax.rem(r + 4 * k, N_RESP), c) for k in (1, 2, 3)]

    barrier = pltpu.get_barrier_semaphore()
    for device in (prev_z, across, sibling, y_side, *x_peers):
        pl.semaphore_signal(barrier, inc=1, device_id=device, device_id_type=MESH)

    kv_copies = [
        pltpu.make_async_copy(
            kv_hbm.at[:, :, pl.ds(g * HEAD_SIZE, HEAD_SIZE)], kv_raw.at[g], kv_sem.at[g]
        )
        for g in range(KEY_VALUE_HEADS)
    ]
    for copy in kv_copies:
        copy.start()
    own_place = pl.ds((core * 8 + pair) * 8, 8)
    own_copy = pltpu.make_async_copy(prompt_hbm, prompt_raw.at[own_place], own_sem)
    own_copy.start()
    q_copy = pltpu.make_async_copy(q_hbm, q, q_sem)
    q_copy.start()

    def pieces(k_from, v_from, slot_of, g, sends, receives, target):
        places = pl.ds(0, ROWS)
        return (
            remote(k_from, other_k.at[slot_of, g, places], sends.at[2 * g], receives.at[2 * g], target),
            remote(v_from, other_v.at[slot_of, g, places], sends.at[2 * g + 1], receives.at[2 * g + 1], target),
        )

    def z_copies(g):
        return pieces(own_k.at[g], own_v.at[g], odd, g, z_send, z_recv, next_z)

    def own_y_copies(g):
        return pieces(own_k.at[g], own_v.at[g], 0, g, y_send, y_recv, across)

    def onward_copies(g):
        k_from = other_k.at[1, g, pl.ds(0, ROWS)]
        v_from = other_v.at[1, g, pl.ds(0, ROWS)]
        return pieces(k_from, v_from, 1, g, y_send, y_recv, across)

    side_pair = pair + 1 - 2 * lax.rem(pair, 2)
    side_place = pl.ds((core * 8 + side_pair) * 8, 8)
    own_rows = prompt_raw.at[own_place]
    side_rows = prompt_raw.at[side_place]
    first = [
        remote(prompt_hbm, own_rows, first_send.at[k], first_recv.at[k], target)
        for k, target in enumerate((y_side, *x_peers))
    ]
    second = [
        remote(side_rows, side_rows, second_send.at[k], second_recv.at[k], target)
        for k, target in enumerate(x_peers)
    ]
    half = prompt_raw.at[pl.ds(core * 64, 64)]
    third = remote(half, half, third_send, third_recv, sibling)

    for g in range(KEY_VALUE_HEADS):
        kv_copies[g].wait()
        both = kv_raw[g].astype(F32)
        own_k[g] = both[:, 0].astype(BF16)
        own_v[g] = both[:, 1].astype(BF16)
        if g == 0:
            pl.semaphore_wait(barrier, 7)
        for copy in z_copies(g):
            copy.start()

        @pl.when(odd == 0)
        def _():
            for copy in own_y_copies(g):
                copy.start()

        if g == 0:
            for copy in first:
                copy.start()

    slot = slot_ref[c]
    live_length = length_ref[0]
    row = lax.broadcasted_iota(jnp.int32, (ROWS, ROWS), 0)
    column = lax.broadcasted_iota(jnp.int32, (ROWS, ROWS), 1)
    near_ok = (column <= row) & (slot * ROWS + column < live_length)
    near_bias[...] = jnp.where(near_ok, 0.0, NEGATIVE_FILL)
    key = lax.broadcasted_iota(jnp.int32, (1, ROWS), 1)

    def other_bias(back):
        source_slot = slot_ref[lax.rem(c + N_CTX - back, N_CTX)]
        ok = (source_slot * ROWS + key < live_length) & (source_slot < slot)
        return jnp.where(ok, 0.0, NEGATIVE_FILL)

    early_bias = jnp.concatenate([other_bias(2 - odd), jnp.zeros((1, PROMPT), F32)], axis=1)
    late_bias = other_bias(1 + odd)
    query = lax.broadcasted_iota(jnp.int32, (ROWS, HEAD_SIZE), 0)
    is_live = slot * ROWS + query < live_length
    lane = lax.broadcasted_iota(jnp.int32, (ROWS, HEAD_SIZE), 1)
    top_all[...] = jnp.zeros_like(top_all)
    total_all[...] = jnp.ones_like(total_all)

    def absorb(g, k_ref, v_ref, width, bias, is_first, is_last):
        k_tile = k_ref.at[g, pl.ds(0, width)]
        v_tile = v_ref.at[g, pl.ds(0, width)]

        def scores(i):
            score[i % 2, :, 0:width] = lax.dot_general(
                q[:, head_columns(g * GROUP + i)], k_tile[...], NT, preferred_element_type=F32
            )

        def soften(i):
            head = g * GROUP + i
            s = score[i % 2, :, 0:width] * LOG2_SCALE + bias()
            peak = jnp.max(s, axis=1, keepdims=True)
            if is_first:
                top = jnp.broadcast_to(peak, (ROWS, HEAD_SIZE))
            else:
                before = top_of[0, head]
                top = jnp.maximum(before, peak)
                top_of[1, head] = jnp.exp2(before - top)
            top_of[0, head] = top
            shift = jnp.concatenate([top] * (width // HEAD_SIZE), axis=1)
            weight[i % 2, :, 0:width] = jnp.exp2(s - shift).astype(BF16)
            if is_last:
                top_all[...] = jnp.where(lane == head, top, top_all[...])

        def weigh(i):
            head = g * GROUP + i
            v = jnp.concatenate([v_tile[...], jnp.ones((width, HEAD_SIZE), BF16)], axis=1)
            added = jnp.dot(weight[i % 2, :, 0:width], v, preferred_element_type=F32)
            if is_first:
                sum_of[head] = added
                return
            rescale = top_of[1, head]
            held = sum_of[head]
            summed = held[:, :HEAD_SIZE] * rescale + added[:, :HEAD_SIZE]
            total = held[:, HEAD_SIZE:] * rescale + added[:, HEAD_SIZE:]
            if not is_last:
                sum_of[head, :, 0:HEAD_SIZE] = summed
                sum_of[head, :, HEAD_SIZE:] = total
                return
            attended = jnp.where(is_live, summed * (1.0 / total), 0.0)
            out[:, head_columns(head)] = attended.astype(BF16)
            total_all[...] = jnp.where(lane == head, total, total_all[...])

        for step in range(GROUP + 2):
            if step < GROUP:
                scores(step)
            if 1 <= step <= GROUP:
                soften(step - 1)
            if step >= 2:
                weigh(step - 2)

    q_copy.wait()
    first[0].wait_recv()
    for copy in second:
        copy.start()

    @pl.loop(0, KEY_VALUE_HEADS)
    def _(g):
        absorb(g, own_k, own_v, ROWS, lambda: near_bias[...], True, False)

    def out_copy(g):
        wide = GROUP * HEAD_SIZE
        columns = pl.ds(pl.multiple_of(g * wide, wide), wide)
        return pltpu.make_async_copy(out.at[:, columns], out_ref.at[:, columns], out_sem.at[g])

    own_copy.wait()
    for copy in (*first[1:], *second):
        copy.wait_recv()
    third.start()
    for copy in (*first, *second):
        copy.wait_send()
    third.wait()
    rows = prompt_raw[...].astype(F32)
    for g in range(KEY_VALUE_HEADS):
        lanes = slice(g * HEAD_SIZE, (g + 1) * HEAD_SIZE)
        other_k[0, g, ROWS:LAST] = rows[:, 0, lanes].astype(BF16)
        other_v[0, g, ROWS:LAST] = rows[:, 1, lanes].astype(BF16)

    @pl.loop(0, KEY_VALUE_HEADS)
    def _(g):
        @pl.when(odd == 0)
        def _():
            for arriving in z_copies(g):
                arriving.wait_recv()

        @pl.when(odd == 1)
        def _():
            for arriving in own_y_copies(g):
                arriving.wait_recv()

        absorb(g, other_k.at[0], other_v.at[0], LAST, lambda: early_bias, False, False)

        @pl.when(odd == 0)
        def _():
            for arriving in onward_copies(g):
                arriving.wait_recv()

        @pl.when(odd == 1)
        def _():
            for arriving, sending in zip(z_copies(g), onward_copies(g), strict=True):
                arriving.wait_recv()
                sending.start()

        absorb(g, other_k.at[1], other_v.at[1], ROWS, lambda: late_bias, False, True)
        out_copy(g).start()

    log_total = ((top_all[...] + jnp.log2(total_all[...])) * LN2).T[:QUERY_HEADS]
    place = lax.broadcasted_iota(jnp.int32, (QUERY_HEADS, ROWS), 1)
    log_ref[...] = jnp.where(slot * ROWS + place < live_length, log_total, 0.0)

    for g in range(KEY_VALUE_HEADS):
        for copy in (*z_copies(g), *own_y_copies(g)):
            copy.wait_send()
        out_copy(g).wait()


def hand_on(attended_in, log_in, attended_out, log_out, held, held_log, in_sem, out_sem):
    pieces = 8
    rows = ROWS // pieces
    places = [pl.ds(i * rows, rows) for i in range(pieces)]
    inward = [pltpu.make_async_copy(attended_in.at[p], held.at[p], in_sem.at[i]) for i, p in enumerate(places)]
    outward = [pltpu.make_async_copy(held.at[p], attended_out.at[p], out_sem.at[i]) for i, p in enumerate(places)]
    inward.append(pltpu.make_async_copy(log_in, held_log, in_sem.at[pieces]))
    outward.append(pltpu.make_async_copy(held_log, log_out, out_sem.at[pieces]))
    for copy in inward:
        copy.start()
    for arriving, leaving in zip(inward, outward, strict=True):
        arriving.wait()
        leaving.start()
    for leaving in outward:
        leaving.wait()


def body(queries, resp_kv, prompt_kv, lengths, block_slot):
    hbm = pl.BlockSpec(memory_space=pltpu.HBM)
    smem = pl.BlockSpec(memory_space=pltpu.SMEM)
    vmem = pl.BlockSpec(memory_space=pltpu.VMEM)
    dma = pltpu.SemaphoreType.DMA
    block = pltpu.VMEM((KEY_VALUE_HEADS, ROWS, HEAD_SIZE), BF16)
    other = pltpu.VMEM((2, KEY_VALUE_HEADS, LAST, HEAD_SIZE), BF16)
    attended, log_total = pl.pallas_call(
        kernel,
        out_shape=(
            jax.ShapeDtypeStruct((ROWS, QUERY_HEADS * HEAD_SIZE), BF16),
            jax.ShapeDtypeStruct((QUERY_HEADS, ROWS), F32),
        ),
        in_specs=[hbm, hbm, hbm, smem, smem],
        out_specs=(hbm, vmem),
        scratch_shapes=[
            pltpu.VMEM((ROWS, QUERY_HEADS * HEAD_SIZE), BF16),
            pltpu.VMEM((KEY_VALUE_HEADS, ROWS, 2, HEAD_SIZE), BF16),
            pltpu.VMEM((PROMPT, 2, KEY_VALUE_HEADS * HEAD_SIZE), BF16),
            block, block, other, other,
            pltpu.VMEM((ROWS, ROWS), F32),
            pltpu.VMEM((2, QUERY_HEADS, ROWS, HEAD_SIZE), F32),
            pltpu.VMEM((QUERY_HEADS, ROWS, 2 * HEAD_SIZE), F32),
            pltpu.VMEM((ROWS, HEAD_SIZE), F32),
            pltpu.VMEM((ROWS, HEAD_SIZE), F32),
            pltpu.VMEM((2, ROWS, LAST), F32),
            pltpu.VMEM((2, ROWS, LAST), BF16),
            pltpu.VMEM((ROWS, QUERY_HEADS * HEAD_SIZE), BF16),
            dma, dma((4,)), dma, dma((8,)), dma((8,)), dma((8,)), dma((8,)),
            dma((4,)), dma((4,)), dma((3,)), dma((3,)), dma, dma, dma((4,)),
        ],
        compiler_params=pltpu.CompilerParams(
            collective_id=0, has_side_effects=True, vmem_limit_bytes=63 * 1024 * 1024
        ),
    )(queries[0], resp_kv[0], prompt_kv[0], lengths, block_slot)
    attended, log_total = pl.pallas_call(
        hand_on,
        out_shape=(
            jax.ShapeDtypeStruct((ROWS, QUERY_HEADS * HEAD_SIZE), BF16),
            jax.ShapeDtypeStruct((QUERY_HEADS, ROWS), F32),
        ),
        in_specs=[hbm, hbm],
        out_specs=(hbm, hbm),
        scratch_shapes=[
            pltpu.VMEM((ROWS, QUERY_HEADS * HEAD_SIZE), BF16),
            pltpu.VMEM((QUERY_HEADS, ROWS), F32),
            dma((9,)), dma((9,)),
        ],
        compiler_params=pltpu.CompilerParams(vmem_limit_bytes=63 * 1024 * 1024),
    )(attended, log_total)
    return attended[None], log_total[None]


def solution(mesh):
    return jax.shard_map(
        body,
        mesh=mesh,
        in_specs=(
            P("resp", "ctx", None),
            P("resp", "ctx", None, None),
            P("ctx", "resp", None, None),
            P("resp"),
            P(),
        ),
        out_specs=(P("resp", "ctx", None), P("resp", None, "ctx")),
        check_vma=False,
    )
```

time: 44.8 us -> 40.2 us (0.90)
  the two profiles are of different devices: /device:TPU:96 before, /device:TPU:2 now
where the time goes in v2:
time: 40.2 us; the launch traced here: 40 us
  Pallas kernels  38.7 us (96%)
  between operations  1.28 us (3%)
    pallas_call x1, Pallas kernels, body(): pl.pallas_call(kernel, out_shape=(jax.ShapeDtypeStruct((ROWS, QUERY_HEADS...  36.3 us
    pallas_call x1, Pallas kernels, body(): pl.pallas_call(hand_on, out_shape=(jax.ShapeDtypeStruct((ROWS, QUERY_HEAD...  2.41 us

profile of v2, /device:TPU:2, one launch (start us, length us, event | category | flops | bytes accessed | tf_op | source)
XLA Modules:
  0.0 40.0 jit_solution(18070318360659563725)
XLA Ops:
  1.3 36.3 %shard_map.68 = (bf16[256,4096]{1,0:T(8,128)(2,1)}, f32[32,256]{1,0:T(8,128)}) custom-call(bf16[256,4096]{1,0:T(8,128)(2,1)} %bitcast.5, bf16[256,2,512]{2,1,0:T(2,128)(2,1)} %bitcast.6, bf16[8,2,512]{2,1,0:T(2,128)(2,1)} %bitcast.7, s32[1]{0:T(128)S(6)} %copy.7.length_ref, s32[32]{0:T(128)} %slot_ref.1), custom_call_target="tpu_custom_call" | custom-call | tf_op jit(solution)/shard_map/pallas_call | solution.py:299
  37.5 2.4 %shard_map.69 = (bf16[256,4096]{1,0:T(8,128)(2,1)}, f32[32,256]{1,0:T(8,128)}) custom-call(bf16[256,4096]{1,0:T(8,128)(2,1)} %get-tuple-element.6.attended_in, f32[32,256]{1,0:T(8,128)} %get-tuple-element.7.log_in), custom_call_target="tpu_custom_call" | custom-call | tf_op jit(solution)/shard_map/pallas_call | solution.py:327

commit v3 on v2

--- a/solution.py
+++ b/solution.py
@@ -15,6 +15,7 @@
 PROMPT = 128
 LAST = ROWS + PROMPT
 N_CTX = 32
+AHEAD = 2
 N_RESP = 16
 NEGATIVE_FILL = -1e30
 LOG2_SCALE = math.log2(math.e) / math.sqrt(HEAD_SIZE)
@@ -125,13 +126,14 @@
         for copy in z_copies(g):
             copy.start()
 
-        @pl.when(odd == 0)
-        def _():
-            for copy in own_y_copies(g):
-                copy.start()
-
         if g == 0:
             for copy in first:
+                copy.start()
+
+    @pl.when(odd == 0)
+    def _():
+        for g in range(KEY_VALUE_HEADS):
+            for copy in own_y_copies(g):
                 copy.start()
 
     slot = slot_ref[c]
@@ -155,7 +157,8 @@
     top_all[...] = jnp.zeros_like(top_all)
     total_all[...] = jnp.ones_like(total_all)
 
-    def absorb(g, k_ref, v_ref, width, bias, is_first, is_last):
+    def absorb(g, k_ref, v_ref, width, bias, is_first, is_last, await_values=None):
+        held_heads = GROUP if is_last else 2
         k_tile = k_ref.at[g, pl.ds(0, width)]
         v_tile = v_ref.at[g, pl.ds(0, width)]
 
@@ -176,14 +179,14 @@
                 top_of[1, head] = jnp.exp2(before - top)
             top_of[0, head] = top
             shift = jnp.concatenate([top] * (width // HEAD_SIZE), axis=1)
-            weight[i % 2, :, 0:width] = jnp.exp2(s - shift).astype(BF16)
+            weight[i % held_heads, :, 0:width] = jnp.exp2(s - shift).astype(BF16)
             if is_last:
                 top_all[...] = jnp.where(lane == head, top, top_all[...])
 
         def weigh(i):
             head = g * GROUP + i
             v = jnp.concatenate([v_tile[...], jnp.ones((width, HEAD_SIZE), BF16)], axis=1)
-            added = jnp.dot(weight[i % 2, :, 0:width], v, preferred_element_type=F32)
+            added = jnp.dot(weight[i % held_heads, :, 0:width], v, preferred_element_type=F32)
             if is_first:
                 sum_of[head] = added
                 return
@@ -199,6 +202,16 @@
             out[:, head_columns(head)] = attended.astype(BF16)
             total_all[...] = jnp.where(lane == head, total, total_all[...])
 
+        if is_last:
+            for step in range(GROUP + 1):
+                if step < GROUP:
+                    scores(step)
+                if step >= 1:
+                    soften(step - 1)
+            await_values()
+            for step in range(GROUP):
+                weigh(step)
+            return
         for step in range(GROUP + 2):
             if step < GROUP:
                 scores(step)
@@ -221,10 +234,19 @@
         columns = pl.ds(pl.multiple_of(g * wide, wide), wide)
         return pltpu.make_async_copy(out.at[:, columns], out_ref.at[:, columns], out_sem.at[g])
 
+    def pass_on(g):
+        @pl.when((odd == 1) & (c >= 2))
+        def _():
+            for arriving, sending in zip(z_copies(g), onward_copies(g), strict=True):
+                arriving.wait_recv()
+                sending.start()
+
+    pass_on(0)
     own_copy.wait()
     for copy in (*first[1:], *second):
         copy.wait_recv()
     third.start()
+    pass_on(1)
     for copy in (*first, *second):
         copy.wait_send()
     third.wait()
@@ -248,18 +270,23 @@
 
         absorb(g, other_k.at[0], other_v.at[0], LAST, lambda: early_bias, False, False)
 
-        @pl.when(odd == 0)
-        def _():
-            for arriving in onward_copies(g):
-                arriving.wait_recv()
-
-        @pl.when(odd == 1)
-        def _():
-            for arriving, sending in zip(z_copies(g), onward_copies(g), strict=True):
-                arriving.wait_recv()
-                sending.start()
-
-        absorb(g, other_k.at[1], other_v.at[1], ROWS, lambda: late_bias, False, True)
+        arriving_far = z_copies(g)
+        passing = onward_copies(g)
+
+        def await_part(part):
+            @pl.when(odd == 0)
+            def _():
+                passing[part].wait_recv()
+
+            @pl.when((odd == 1) & ((c < 2) | (g >= AHEAD)))
+            def _():
+                arriving_far[part].wait_recv()
+                passing[part].start()
+
+        await_part(0)
+        absorb(
+            g, other_k.at[1], other_v.at[1], ROWS, lambda: late_bias, False, True, lambda: await_part(1)
+        )
         out_copy(g).start()
 
     log_total = ((top_all[...] + jnp.log2(total_all[...])) * LN2).T[:QUERY_HEADS]
@@ -315,7 +342,7 @@
             pltpu.VMEM((ROWS, HEAD_SIZE), F32),
             pltpu.VMEM((ROWS, HEAD_SIZE), F32),
             pltpu.VMEM((2, ROWS, LAST), F32),
-            pltpu.VMEM((2, ROWS, LAST), BF16),
+            pltpu.VMEM((GROUP, ROWS, LAST), BF16),
             pltpu.VMEM((ROWS, QUERY_HEADS * HEAD_SIZE), BF16),
             dma, dma((4,)), dma, dma((8,)), dma((8,)), dma((8,)), dma((8,)),
             dma((4,)), dma((4,)), dma((3,)), dma((3,)), dma, dma, dma((4,)),

time: 40.2 us -> 39.3 us (0.978)
  Pallas kernels: 38.7 us -> 37.8 us
    pallas_call x1, Pallas kernels: 36.3 us -> 35.4 us  [body(): pl.pallas_call(kernel, out_shape=(jax.ShapeDtypeStruct((ROWS, QUERY_HEADS...]
where the time goes in v3:
time: 39.3 us; the launch traced here: 39.1 us
  Pallas kernels  37.8 us (96%)
  between operations  1.28 us (3%)
    pallas_call x1, Pallas kernels, body(): pl.pallas_call(kernel, out_shape=(jax.ShapeDtypeStruct((ROWS, QUERY_HEADS...  35.4 us
    pallas_call x1, Pallas kernels, body(): pl.pallas_call(hand_on, out_shape=(jax.ShapeDtypeStruct((ROWS, QUERY_HEAD...  2.41 us

profile of v3, /device:TPU:2, one launch (start us, length us, event | category | flops | bytes accessed | tf_op | source)
XLA Modules:
  0.0 39.1 jit_solution(8437956857755754623)
XLA Ops:
  1.3 35.4 %shard_map.68 = (bf16[256,4096]{1,0:T(8,128)(2,1)}, f32[32,256]{1,0:T(8,128)}) custom-call(bf16[256,4096]{1,0:T(8,128)(2,1)} %bitcast.5, bf16[256,2,512]{2,1,0:T(2,128)(2,1)} %bitcast.6, bf16[8,2,512]{2,1,0:T(2,128)(2,1)} %bitcast.7, s32[1]{0:T(128)S(6)} %copy.7.length_ref, s32[32]{0:T(128)} %slot_ref.1), custom_call_target="tpu_custom_call" | custom-call | tf_op jit(solution)/shard_map/pallas_call | solution.py:326
  36.7 2.4 %shard_map.69 = (bf16[256,4096]{1,0:T(8,128)(2,1)}, f32[32,256]{1,0:T(8,128)}) custom-call(bf16[256,4096]{1,0:T(8,128)(2,1)} %get-tuple-element.6.attended_in, f32[32,256]{1,0:T(8,128)} %get-tuple-element.7.log_in), custom_call_target="tpu_custom_call" | custom-call | tf_op jit(solution)/shard_map/pallas_call | solution.py:354

commit v4 on v3

--- a/solution.py
+++ b/solution.py
@@ -84,10 +84,13 @@
     q_copy.start()
 
     def pieces(k_from, v_from, slot_of, g, sends, receives, target):
-        places = pl.ds(0, ROWS)
-        return (
-            remote(k_from, other_k.at[slot_of, g, places], sends.at[2 * g], receives.at[2 * g], target),
-            remote(v_from, other_v.at[slot_of, g, places], sends.at[2 * g + 1], receives.at[2 * g + 1], target),
+        parts = [(k_from, other_k.at[slot_of, g, pl.ds(0, ROWS)])]
+        for start in (0, ROWS // 2):
+            places = pl.ds(start, ROWS // 2)
+            parts.append((v_from.at[places], other_v.at[slot_of, g, places]))
+        return tuple(
+            remote(src, dst, sends.at[3 * g + k], receives.at[3 * g + k], target)
+            for k, (src, dst) in enumerate(parts)
         )
 
     def z_copies(g):
@@ -283,9 +286,13 @@
                 arriving_far[part].wait_recv()
                 passing[part].start()
 
+        def await_values():
+            await_part(1)
+            await_part(2)
+
         await_part(0)
         absorb(
-            g, other_k.at[1], other_v.at[1], ROWS, lambda: late_bias, False, True, lambda: await_part(1)
+            g, other_k.at[1], other_v.at[1], ROWS, lambda: late_bias, False, True, await_values
         )
         out_copy(g).start()
 
@@ -344,7 +351,7 @@
             pltpu.VMEM((2, ROWS, LAST), F32),
             pltpu.VMEM((GROUP, ROWS, LAST), BF16),
             pltpu.VMEM((ROWS, QUERY_HEADS * HEAD_SIZE), BF16),
-            dma, dma((4,)), dma, dma((8,)), dma((8,)), dma((8,)), dma((8,)),
+            dma, dma((4,)), dma, dma((12,)), dma((12,)), dma((12,)), dma((12,)),
             dma((4,)), dma((4,)), dma((3,)), dma((3,)), dma, dma, dma((4,)),
         ],
         compiler_params=pltpu.CompilerParams(

time: 39.3 us -> 39.4 us (level)
  no operation moved by 1% of the time
where the time goes in v4:
time: 39.4 us; the launch traced here: 39.2 us
  Pallas kernels  37.9 us (96%)
  between operations  1.28 us (3%)
    pallas_call x1, Pallas kernels, body(): pl.pallas_call(kernel, out_shape=(jax.ShapeDtypeStruct((ROWS, QUERY_HEADS...  35.5 us
    pallas_call x1, Pallas kernels, body(): pl.pallas_call(hand_on, out_shape=(jax.ShapeDtypeStruct((ROWS, QUERY_HEAD...  2.41 us

profile of v4, /device:TPU:2, one launch (start us, length us, event | category | flops | bytes accessed | tf_op | source)
XLA Modules:
  0.0 39.2 jit_solution(13399779957717518531)
XLA Ops:
  1.3 35.5 %shard_map.68 = (bf16[256,4096]{1,0:T(8,128)(2,1)}, f32[32,256]{1,0:T(8,128)}) custom-call(bf16[256,4096]{1,0:T(8,128)(2,1)} %bitcast.5, bf16[256,2,512]{2,1,0:T(2,128)(2,1)} %bitcast.6, bf16[8,2,512]{2,1,0:T(2,128)(2,1)} %bitcast.7, s32[1]{0:T(128)S(6)} %copy.7.length_ref, s32[32]{0:T(128)} %slot_ref.1), custom_call_target="tpu_custom_call" | custom-call | tf_op jit(solution)/shard_map/pallas_call | solution.py:333
  36.8 2.4 %shard_map.69 = (bf16[256,4096]{1,0:T(8,128)(2,1)}, f32[32,256]{1,0:T(8,128)}) custom-call(bf16[256,4096]{1,0:T(8,128)(2,1)} %get-tuple-element.6.attended_in, f32[32,256]{1,0:T(8,128)} %get-tuple-element.7.log_in), custom_call_target="tpu_custom_call" | custom-call | tf_op jit(solution)/shard_map/pallas_call | solution.py:361
